TPU v7x, 128 devices: a whole 4x4x4 slice. The times are simulated.
128 devices in a mesh: ctx: 64 (over y, x, z), tp: 2 (over core).
Axes of the slice: x: 4, y: 4, z: 4, core: 2. Of those that a mesh axis runs over, the one named last changes fastest.
Arguments:
- tokens: bfloat16 [64, 2, 80, 896], P('ctx', None, 'tp'), may hold values from -16 to 16
- gain_attn: float32 [896], replicated, may hold values from 0.5 to 1.5
- query_projection_weight: bfloat16 [896, 896], P(None, 'tp'), may hold values from -0.1875 to 0.1875
- query_bias_vector: float32 [896], P('tp'), may hold values from -3 to 3
- key_projection_weight: bfloat16 [896, 128], P(None, 'tp'), may hold values from -0.1875 to 0.1875
- key_bias_vector: float32 [128], P('tp'), may hold values from -4 to 4
- value_projection_weight: bfloat16 [896, 128], P(None, 'tp'), may hold values from -0.1875 to 0.1875
- value_bias_vector: float32 [128], P('tp'), may hold values from -3 to 3
- w_output: bfloat16 [896, 896], P('tp'), may hold values from -0.75 to 0.75
- gain_mlp: float32 [896], replicated, may hold values from 0.5 to 1.5
- w_gate: bfloat16 [896, 4864], P(None, 'tp'), may hold values from -0.1875 to 0.1875
- w_up: bfloat16 [896, 4864], P(None, 'tp'), may hold values from -0.1875 to 0.1875
- w_down: bfloat16 [4864, 896], P('tp'), may hold values from -0.078125 to 0.078125
- cotangent: bfloat16 [64, 2, 80, 896], P('ctx', None, 'tp'), may hold values from -16 to 16
Outputs:
- mixed: bfloat16 [64, 2, 80, 896], P('ctx', None, 'tp')
- grad_tokens: bfloat16 [64, 2, 80, 896], P('ctx', None, 'tp')
- grad_gain_attn: float32 [896], replicated
- grad_w_query: float32 [896, 896], P('ctx', 'tp')
- grad_b_query: float32 [896], replicated
- grad_w_key: float32 [896, 128], P('ctx', 'tp')
- grad_b_key: float32 [128], replicated
- grad_w_value: float32 [896, 128], P('ctx', 'tp')
- grad_b_value: float32 [128], replicated
- grad_w_output: float32 [896, 896], P('tp', 'ctx')
- grad_gain_mlp: float32 [896], replicated
- grad_w_gate: float32 [896, 4864], P('ctx', 'tp')
- grad_w_up: float32 [896, 4864], P('ctx', 'tp')
- grad_w_down: float32 [4864, 896], P('tp', 'ctx')
All inputs are finite; a program needn't handle non-finite values.
Results may differ from a plain program's by a relative error of at most 0.025.
Values may be sent and summed in bfloat16 or wider, within the bound.
No kernel may reach another device: no remote copies, remote signals or barrier semaphores. Data moves between devices by JAX's collectives and lax.ppermute only.
A program may use at most 192 MiB of HBM per device.

v0:
```python
import math

import jax
import jax.numpy as jnp
from jax import lax
from jax.sharding import Mesh
from jax.sharding import PartitionSpec as P

QUERY_HEADS = 14
KEY_VALUE_HEADS = 2
HEAD_DIM = 64
CTX = ("ctx_0", "ctx_1", "ctx_2")


EPS = 1e-06
THETA = 1000000.0
NEG_FILL = -1e30


def side_by_side(arrays, axis, dim, along):
    widths = [a.shape[along] for a in arrays]
    both = jnp.concatenate(arrays, axis=along)
    result = lax.all_gather(both, axis, axis=dim, tiled=True)
    return tuple(jnp.split(result, [sum(widths[:k]) for k in range(1, len(widths))], axis=along))


def from_everyone(shard, axis):
    size = lax.axis_size(axis)
    return lax.all_to_all(
        jnp.broadcast_to(shard[None], (size, *shard.shape)), axis, 0, 0, tiled=True
    )


def in_order(blocks, dim):
    dims = list(blocks.shape[1:])
    dims[dim] *= blocks.shape[0]
    return jnp.moveaxis(blocks, 0, dim).reshape(dims)


def collect(shard, axis, dim):
    blocks = from_everyone(shard, axis)
    return in_order(blocks, dim)


def split_up(shard, dim, size):
    dims = shard.shape
    blocks = shard.reshape(*dims[:dim], size, dims[dim] // size, *dims[dim + 1 :])
    return jnp.moveaxis(blocks, dim, 0)


def summed_on_arrival(shard, axis, dim):
    size = lax.axis_size(axis)
    blocks = lax.all_to_all(split_up(shard, dim, size), axis, 0, 0, tiled=True)
    return jnp.sum(blocks.astype(jnp.float32), axis=0)


def sum_at_owner(shard, axis, dim):
    blocks = split_up(shard, dim, lax.axis_size(axis))
    arrived = lax.all_to_all(blocks, axis, split_axis=0, concat_axis=0, tiled=True)
    return arrived.sum(axis=0)


def sum_in_two_steps(shard, axes, dim):
    far, near = axes
    blocks = split_up(shard, dim, lax.axis_size(far))
    nearer = sum_at_owner(blocks, near, dim + 1)
    arrived = lax.all_to_all(nearer, far, split_axis=0, concat_axis=0, tiled=True)
    return arrived.sum(axis=0)


def in_one_piece(arrays, axis, dim, along):
    ends, at = ([], 0)
    for a in arrays[:-1]:
        at += a.shape[along]
        ends.append(at)
    both = jnp.concatenate(arrays, axis=along)
    return tuple(jnp.split(sum_in_two_steps(both, axis, dim), ends, axis=along))


def sum_packed(arrays, axis, dims):
    size = lax.axis_size(axis)
    blocks = [split_up(a, dim, size) for a, dim in zip(arrays, dims)]
    lines = jnp.concatenate([b.reshape(size, -1) for b in blocks], axis=1)
    rows = max(16, -(-lines.shape[1] // 1024) * 8)
    lines = jnp.pad(lines, ((0, 0), (0, rows * 128 - lines.shape[1]))).reshape(-1, 128)
    ravelled, at, done = (lax.psum_scatter(lines, axis, tiled=True).reshape(-1), 0, [])
    for b in blocks:
        part = b[0]
        done.append(ravelled[at : at + part.size].reshape(part.shape))
        at += part.size
    return tuple(done)


def in_one_piece_2(arrays, axis, dim, along):
    both = jnp.concatenate(arrays, axis=along)
    result, at, done = (lax.psum_scatter(both, axis, scatter_dimension=dim, tiled=True), 0, [])
    for a in arrays:
        done.append(lax.slice_in_dim(result, at, at + a.shape[along], axis=along))
        at += a.shape[along]
    return tuple(done)


def over_copies(shard, axis):
    everything = from_everyone(shard, axis)
    return jnp.sum(everything, axis=0)


def over_axes(shard, axes):
    far, near = axes
    return over_copies(over_copies(shard, near), far)


def packed_total(arrays, axis):
    ravelled, at, done = (jnp.concatenate([a.reshape(-1) for a in arrays]), 0, [])
    total = over_axes(ravelled, axis)
    for a in arrays:
        done.append(total[at : at + a.size].reshape(a.shape))
        at += a.size
    return tuple(done)


def rms_forward(rows, gain):
    inverse = lax.rsqrt(jnp.mean(rows * rows, axis=-1, keepdims=True) + EPS)
    return (rows * inverse * gain, inverse)


def rms_backward(rows, inverse, gain, grad_out):
    weighted = grad_out * gain
    inner = jnp.mean(rows * weighted, axis=-1, keepdims=True)
    grad_rows = inverse * weighted - rows * (inverse * inverse * inverse) * inner
    grad_gain = jnp.sum(grad_out * rows * inverse, axis=0)
    return (grad_rows, grad_gain)


def token_places(indices, block_size, ctx_count):
    shard_index = indices // (2 * block_size)
    within_pair = indices % (2 * block_size)
    offset_rows = within_pair % block_size
    early_place = shard_index * block_size + offset_rows
    late_place = (2 * ctx_count - 1 - shard_index) * block_size + offset_rows
    return jnp.where(within_pair < block_size, early_place, late_place)


def rope_tables(token_positions, head_size):
    freqs = 1.0 / THETA ** (jnp.arange(0, head_size, 2).astype(jnp.float32) / head_size)
    angles = token_positions.astype(jnp.float32)[:, None] * freqs[None, :]
    return (jnp.cos(angles), jnp.sin(angles))


def table_shape(vectors, cosine, sine):
    shape_parts = (vectors.shape[0],) + (1,) * (vectors.ndim - 2) + (vectors.shape[-1] // 2,)
    return (cosine.reshape(shape_parts), sine.reshape(shape_parts))


def rotate(vectors, cosine, sine):
    cosine_part, sine_part = table_shape(vectors, cosine, sine)
    leading, trailing = jnp.split(vectors, 2, axis=-1)
    return jnp.concatenate(
        [
            leading * cosine_part - trailing * sine_part,
            trailing * cosine_part + leading * sine_part,
        ],
        axis=-1,
    )


def unrotate(grads_in, cosine, sine):
    cosine_part, sine_part = table_shape(grads_in, cosine, sine)
    leading, trailing = jnp.split(grads_in, 2, axis=-1)
    return jnp.concatenate(
        [
            leading * cosine_part + trailing * sine_part,
            trailing * cosine_part - leading * sine_part,
        ],
        axis=-1,
    )


def fetch_keys(key_part, value_part):
    return side_by_side((key_part, value_part), CTX, 0, 1)


def local(
    tokens,
    gain_attn,
    query_projection_weight,
    query_bias_vector,
    key_projection_weight,
    key_bias_vector,
    value_projection_weight,
    value_bias_vector,
    w_output,
    gain_mlp,
    w_gate,
    w_up,
    w_down,
    cotangent,
):
    ctx_count = lax.axis_size(CTX)
    ctx_index = lax.axis_index(CTX)
    tp_count = lax.axis_size("tp")
    tp_index = lax.axis_index("tp")
    half_rows = tokens.shape[2]
    block_size = half_rows * tp_count
    model_width = tokens.shape[3]
    own_rows = 2 * block_size
    kv_local = key_projection_weight.shape[1] // HEAD_DIM
    query_group_width = QUERY_HEADS // KEY_VALUE_HEADS
    local_heads = query_projection_weight.shape[1] // HEAD_DIM
    total_keys = own_rows * ctx_count
    key_block = math.gcd(total_keys, 512)
    key_blocks = total_keys // key_block
    scale_factor = 1.0 / math.sqrt(HEAD_DIM)
    stacked_shape = (1, 2, block_size, model_width)
    own_places = token_places(ctx_index * own_rows + jnp.arange(own_rows), block_size, ctx_count)
    key_places = token_places(jnp.arange(total_keys), block_size, ctx_count).reshape(
        key_blocks, key_block
    )
    cosine, sine = rope_tables(own_places, HEAD_DIM)
    x_rows = tokens.astype(jnp.float32).reshape(-1, model_width)
    normalized_rows, inverse_attn = rms_forward(x_rows, gain_attn)
    normed_all = collect(
        normalized_rows.astype(jnp.bfloat16).reshape(tokens.shape), "tp", 2
    ).reshape(own_rows, model_width)
    query_pre = (
        jnp.dot(normed_all, query_projection_weight, preferred_element_type=jnp.float32)
        + query_bias_vector
    )
    key_pre = (
        jnp.dot(normed_all, key_projection_weight, preferred_element_type=jnp.float32)
        + key_bias_vector
    )
    value_pre = (
        jnp.dot(normed_all, value_projection_weight, preferred_element_type=jnp.float32)
        + value_bias_vector
    )
    query_low = rotate(
        query_pre.reshape(own_rows, kv_local, query_group_width, HEAD_DIM), cosine, sine
    ).astype(jnp.bfloat16)
    key_low = rotate(key_pre.reshape(own_rows, kv_local, HEAD_DIM), cosine, sine).astype(
        jnp.bfloat16
    )
    value_low = value_pre.reshape(own_rows, kv_local, HEAD_DIM).astype(jnp.bfloat16)
    key_all, value_all = fetch_keys(key_low, value_low)

    def masked_scores(key_piece, place_piece):
        scores = (
            jnp.einsum("qkgd,skd->kgqs", query_low, key_piece, preferred_element_type=jnp.float32)
            * scale_factor
        )
        allowed = own_places[:, None] >= place_piece[None, :]
        return jnp.where(allowed, scores, NEG_FILL)

    def forward_block(carry, pieces):
        row_max, row_total, accum = carry
        key_piece, value_piece, place_piece = pieces
        scores = masked_scores(key_piece, place_piece)
        new_max = jnp.maximum(row_max, jnp.max(scores, axis=-1))
        shrink = jnp.exp(row_max - new_max)
        exponent = jnp.exp(scores - new_max[..., None])
        row_total = row_total * shrink + jnp.sum(exponent, axis=-1)
        accum = accum * shrink[..., None] + jnp.einsum(
            "kgqs,skd->kgqd",
            exponent.astype(jnp.bfloat16),
            value_piece,
            preferred_element_type=jnp.float32,
        )
        return ((new_max, row_total, accum), None)

    start_max = jnp.full((kv_local, query_group_width, own_rows), NEG_FILL, jnp.float32)
    start_total = jnp.zeros((kv_local, query_group_width, own_rows), jnp.float32)
    start_accum = jnp.zeros((kv_local, query_group_width, own_rows, HEAD_DIM), jnp.float32)
    pieces_fwd = (
        key_all.reshape(key_blocks, key_block, kv_local, HEAD_DIM),
        value_all.reshape(key_blocks, key_block, kv_local, HEAD_DIM),
        key_places,
    )
    (row_max, row_total, accum), unused = lax.scan(
        forward_block, (start_max, start_total, start_accum), pieces_fwd
    )
    out_heads = accum / row_total[..., None]
    log_total = row_max + jnp.log(row_total)
    attended_low = (
        jnp.transpose(out_heads, (2, 0, 1, 3))
        .reshape(own_rows, local_heads * HEAD_DIM)
        .astype(jnp.bfloat16)
    )
    attn_term = jnp.dot(attended_low, w_output, preferred_element_type=jnp.float32).reshape(
        stacked_shape
    )
    attn_rows_own = summed_on_arrival(attn_term.astype(jnp.bfloat16), "tp", 2).reshape(
        -1, model_width
    )
    hidden_rows = x_rows + attn_rows_own
    normed_mlp, inverse_mlp = rms_forward(hidden_rows, gain_mlp)
    normed_mlp_all = collect(
        normed_mlp.astype(jnp.bfloat16).reshape(tokens.shape), "tp", 2
    ).reshape(own_rows, model_width)
    gate_rows = jnp.dot(normed_mlp_all, w_gate, preferred_element_type=jnp.float32)
    up_rows = jnp.dot(normed_mlp_all, w_up, preferred_element_type=jnp.float32)
    sigmoid_gate = jax.nn.sigmoid(gate_rows)
    silu_gate = gate_rows * sigmoid_gate
    activation = (silu_gate * up_rows).astype(jnp.bfloat16)
    mlp_term = jnp.dot(activation, w_down, preferred_element_type=jnp.float32).reshape(
        stacked_shape
    )
    mlp_rows_own = summed_on_arrival(mlp_term.astype(jnp.bfloat16), "tp", 2).reshape(
        -1, model_width
    )
    mixed = (hidden_rows + mlp_rows_own).astype(jnp.bfloat16).reshape(tokens.shape)
    grad_out_all = collect(cotangent, "tp", 2).reshape(own_rows, model_width)
    grad_w_down = jnp.einsum(
        "rf,rd->fd", activation, grad_out_all, preferred_element_type=jnp.float32
    )
    grad_act = jnp.einsum("rd,fd->rf", grad_out_all, w_down, preferred_element_type=jnp.float32)
    grad_gate = (
        grad_act * up_rows * sigmoid_gate * (1.0 + gate_rows * (1.0 - sigmoid_gate))
    ).astype(jnp.bfloat16)
    grad_up = (grad_act * silu_gate).astype(jnp.bfloat16)
    grad_w_gate = jnp.einsum(
        "rd,rf->df", normed_mlp_all, grad_gate, preferred_element_type=jnp.float32
    )
    grad_w_up = jnp.einsum("rd,rf->df", normed_mlp_all, grad_up, preferred_element_type=jnp.float32)
    grad_normed_mlp = jnp.einsum(
        "rf,df->rd", grad_gate, w_gate, preferred_element_type=jnp.float32
    ) + jnp.einsum("rf,df->rd", grad_up, w_up, preferred_element_type=jnp.float32)
    grad_normed_mlp = summed_on_arrival(
        grad_normed_mlp.reshape(stacked_shape).astype(jnp.bfloat16), "tp", 2
    ).reshape(-1, model_width)
    grad_hidden_part, grad_gain_mlp = rms_backward(
        hidden_rows, inverse_mlp, gain_mlp, grad_normed_mlp
    )
    grad_hidden = cotangent.astype(jnp.float32).reshape(-1, model_width) + grad_hidden_part
    grad_attn_all = collect(
        grad_hidden.astype(jnp.bfloat16).reshape(tokens.shape), "tp", 2
    ).reshape(own_rows, model_width)
    grad_w_output = jnp.einsum(
        "rq,rd->qd", attended_low, grad_attn_all, preferred_element_type=jnp.float32
    )
    grad_attended = jnp.einsum(
        "rd,qd->rq", grad_attn_all, w_output, preferred_element_type=jnp.float32
    ).astype(jnp.bfloat16)
    grad_heads = grad_attended.reshape(own_rows, kv_local, query_group_width, HEAD_DIM)
    correction = jnp.sum(
        jnp.transpose(grad_heads.astype(jnp.float32), (1, 2, 0, 3)) * out_heads, axis=-1
    )
    key_back, value_back = (key_all, value_all)

    def backward_block(grad_query, pieces):
        key_piece, value_piece, place_piece = pieces
        scores = masked_scores(key_piece, place_piece)
        attn_probs = jnp.exp(scores - log_total[..., None])
        grad_probs = jnp.einsum(
            "qkgd,skd->kgqs", grad_heads, value_piece, preferred_element_type=jnp.float32
        )
        grad_scores = (attn_probs * (grad_probs - correction[..., None])).astype(jnp.bfloat16)
        grad_query = grad_query + jnp.einsum(
            "kgqs,skd->qkgd", grad_scores, key_piece, preferred_element_type=jnp.float32
        )
        grad_key_piece = (
            jnp.einsum("kgqs,qkgd->skd", grad_scores, query_low, preferred_element_type=jnp.float32)
            * scale_factor
        )
        grad_value_piece = jnp.einsum(
            "kgqs,qkgd->skd",
            attn_probs.astype(jnp.bfloat16),
            grad_heads,
            preferred_element_type=jnp.float32,
        )
        return (grad_query, (grad_key_piece, grad_value_piece))

    pieces_back = (
        key_back.reshape(key_blocks, key_block, kv_local, HEAD_DIM),
        value_back.reshape(key_blocks, key_block, kv_local, HEAD_DIM),
        key_places,
    )
    start_query = jnp.zeros((own_rows, kv_local, query_group_width, HEAD_DIM), jnp.float32)
    grad_query, (grad_key_stack, grad_value_stack) = lax.scan(
        backward_block, start_query, pieces_back
    )
    grad_key_whole = grad_key_stack.reshape(total_keys, kv_local * HEAD_DIM)
    grad_value_whole = grad_value_stack.reshape(total_keys, kv_local * HEAD_DIM)
    grad_key_own, grad_value_own = in_one_piece(
        (grad_key_whole, grad_value_whole), ("ctx_0", ("ctx_1", "ctx_2")), 0, 1
    )
    grad_query_low = (
        unrotate(grad_query * scale_factor, cosine, sine)
        .reshape(own_rows, local_heads * HEAD_DIM)
        .astype(jnp.bfloat16)
    )
    grad_key_low = (
        unrotate(grad_key_own.reshape(own_rows, kv_local, HEAD_DIM), cosine, sine)
        .reshape(own_rows, kv_local * HEAD_DIM)
        .astype(jnp.bfloat16)
    )
    grad_value_low = grad_value_own.astype(jnp.bfloat16)
    grad_w_query = jnp.einsum(
        "rd,rq->dq", normed_all, grad_query_low, preferred_element_type=jnp.float32
    )
    grad_w_key = jnp.einsum(
        "rd,rq->dq", normed_all, grad_key_low, preferred_element_type=jnp.float32
    )
    grad_w_value = jnp.einsum(
        "rd,rq->dq", normed_all, grad_value_low, preferred_element_type=jnp.float32
    )
    grad_b_query = jnp.sum(grad_query_low.astype(jnp.float32), axis=0)
    grad_b_key = jnp.sum(grad_key_low.astype(jnp.float32), axis=0)
    grad_b_value = jnp.sum(grad_value_low.astype(jnp.float32), axis=0)
    grad_normed_attn = jnp.einsum(
        "rq,dq->rd", grad_query_low, query_projection_weight, preferred_element_type=jnp.float32
    )
    grad_normed_attn = grad_normed_attn + jnp.einsum(
        "rq,dq->rd", grad_key_low, key_projection_weight, preferred_element_type=jnp.float32
    )
    grad_normed_attn = grad_normed_attn + jnp.einsum(
        "rq,dq->rd", grad_value_low, value_projection_weight, preferred_element_type=jnp.float32
    )
    grad_normed_attn = summed_on_arrival(
        grad_normed_attn.reshape(stacked_shape).astype(jnp.bfloat16), "tp", 2
    ).reshape(-1, model_width)
    grad_x_part, grad_gain_attn = rms_backward(x_rows, inverse_attn, gain_attn, grad_normed_attn)
    grad_tokens = (grad_hidden + grad_x_part).astype(jnp.bfloat16).reshape(tokens.shape)
    query_shard, key_shard, value_shard, gate_shard, up_shard = sum_packed(
        (grad_w_query, grad_w_key, grad_w_value, grad_w_gate, grad_w_up), CTX, (0, 0, 0, 0, 0)
    )
    output_shard, down_shard = in_one_piece_2((grad_w_output, grad_w_down), CTX, 1, 0)
    query_width = local_heads * HEAD_DIM
    kv_width = kv_local * HEAD_DIM
    full_query = lax.dynamic_update_slice(
        jnp.zeros((query_width * tp_count,), jnp.float32), grad_b_query, (tp_index * query_width,)
    )
    full_key = lax.dynamic_update_slice(
        jnp.zeros((kv_width * tp_count,), jnp.float32), grad_b_key, (tp_index * kv_width,)
    )
    full_value = lax.dynamic_update_slice(
        jnp.zeros((kv_width * tp_count,), jnp.float32), grad_b_value, (tp_index * kv_width,)
    )
    gain_attn_sum, gain_mlp_sum, query_bias_sum, key_bias_sum, value_bias_sum = packed_total(
        (grad_gain_attn, grad_gain_mlp, full_query, full_key, full_value),
        (("ctx_0", "ctx_1"), ("ctx_2", "tp")),
    )
    return (
        mixed,
        grad_tokens,
        gain_attn_sum,
        query_shard,
        query_bias_sum,
        key_shard,
        key_bias_sum,
        value_shard,
        value_bias_sum,
        output_shard,
        gain_mlp_sum,
        gate_shard,
        up_shard,
        down_shard,
    )


def solution(mesh):
    split = Mesh(mesh.devices.reshape(4, 4, 4, mesh.shape["tp"]), ("ctx_0", "ctx_1", "ctx_2", "tp"))
    return jax.shard_map(
        local,
        mesh=split,
        in_specs=(
            P(CTX, None, "tp", None),
            P(),
            P(None, "tp"),
            P("tp"),
            P(None, "tp"),
            P("tp"),
            P(None, "tp"),
            P("tp"),
            P("tp", None),
            P(),
            P(None, "tp"),
            P(None, "tp"),
            P("tp", None),
            P(CTX, None, "tp", None),
        ),
        out_specs=(
            P(CTX, None, "tp", None),
            P(CTX, None, "tp", None),
            P(),
            P(CTX, "tp"),
            P(),
            P(CTX, "tp"),
            P(),
            P(CTX, "tp"),
            P(),
            P("tp", CTX),
            P(),
            P(CTX, "tp"),
            P(CTX, "tp"),
            P("tp", CTX),
        ),
        check_vma=False,
    )
```

profile of v0, /device:TPU:0, one launch (start us, length us, event | category | flops | bytes accessed | tf_op | source)
XLA Modules:
  0.0 1150.3 jit_solution(265577992931423013)
XLA Ops:
  25.8 65.7 %all-gather.2.cloned.1.call-done = bf16[10240,2,64]{2,1,0:T(2,128)(2,1)} async-done(((bf16[160,2,64]{2,1,0:T(2,128)(2,1)}), bf16[10240,2,64]{2,1,0:T(2,128)(2,1)}) %all-gather.2.cloned.1.call-update) | async-done | bytes 2621456 | tf_op jit(solution)/shard_map/all_gather | solution.py:23
  91.6 11.4 fusion.118
  103.0 4.0 copy.210
  107.0 4.0 copy.171
  111.0 4.3 copy.211
  115.3 4.0 copy.172
  119.3 154.5 %while.30 = (s32[]{:T(128)}, f32[1,7,160]{2,1,0:T(8,128)}, f32[1,7,160]{2,1,0:T(8,128)}, f32[1,7,160,64]{2,3,1,0:T(8,128)}, s32[20,512]{1,0:T(8,128)}, /*index=5...) while((s32[]{:T(128)}, f32[1,7,160]{2,1,0:T(8,128)}, ...), condition=%wide.region_4.5_spmd.clone, body=%wide.region_1.4_spmd.clone.sunk | while | flops 153416320 | bytes 10483741 | solution.py:278
  275.4 3.9 all_to_all.62
  279.7 4.7 all_to_all.63
  303.7 4.2 all_to_all.64
  310.3 327.4 %while.31 = (s32[]{:T(128)}, f32[160,1,7,64]{0,3,2,1:T(8,128)S(1)}, f32[20,512,1,64]{1,0,3,2:T(8,128)}, f32[20,512,1,64]{1,0,3,2:T(8,128)}, bf16[20,512,1,64]{1,...) while((s32[]{:T(128)}, f32[160,1,7,64]{0,3,2,1:T(8,128)S(1)}, ...), condition=%wide.region_12.13_spmd.clone, body=%wide.region_11.12_spmd.clone.sunk | while | flops 372998208 | bytes 22418000 | solution.py:378
  333.0 3.8 dynamic_update_slice.23
  415.0 3.8 dynamic_update_slice.23
  637.7 5.5 concatenate.75
  643.2 5.4 concatenate.74
  648.7 8.7 maximum_bitcast_fusion
  657.3 9.1 copy.185
  666.4 5.1 all-to-all-start.7
  677.4 4.8 fusion.126
  682.2 9.9 reshape_reshape.35
  695.2 5.9 pad_maximum_fusion
  703.9 48.8 %all-to-all-done.7 = f32[16,4,160,128]{3,2,1,0:T(8,128)} async-done(((f32[16,4,160,128]{3,2,1,0:T(8,128)}), f32[16,4,160,128]{3,2,1,0:T(8,128)}, u32[]{:S(2)}, u32[]{:S(2)}) %all-to-all-start.7) | async-done | bytes 5242912 | tf_op jit(solution)/shard_map/all_to_all | solution.py:59
  759.7 4.8 fusion.127
  764.4 9.9 reshape_reshape.36
  777.3 7.9 constant_dynamic-update-slice_fusion.2
  785.2 4.0 constant_dynamic-update-slice_fusion.1
  789.1 15.0 %pad.4 = f32[64,76800]{1,0:T(8,128)} pad(f32[64,76160]{1,0:T(8,128)} %constant_dynamic-update-slice_fusion.1, f32[]{:T(128)} %constant.122.clone.1), padding=0_0x0_640 | pad | bytes 39157764 | tf_op jit(solution)/shard_map/jit(_pad)/pad | solution.py:85
  804.1 16.0 %reshape.814 = f32[38400,128]{1,0:T(8,128)} reshape(f32[64,76800]{1,0:T(8,128)} %pad.4) | data formatting | bytes 39321600 | tf_op jit(solution)/shard_map/reshape | solution.py:85
  843.2 7.1 all-to-all-done.10
  851.1 14.9 %all-to-all-start.11 = ((f32[16,1,2944]{2,1,0:T(1,128)}), f32[16,1,2944]{2,1,0:T(1,128)S(1)}, u32[]{:S(2)}, u32[]{:S(2)}) async-start(f32[16,1,2944]{2,1,0:T(1,128)} %broadcast_in_dim.104), calls=%async_computation.11 | async-start | bytes 376832 | tf_op jit(solution)/shard_map/all_to_all | solution.py:29
  867.0 9.8 all-to-all-done.11
  878.1 254.1 %all-reduce.6.cloned.1.call-done = (f32[38400,128]{1,0:T(8,128)}, f32[2880,896]{1,0:T(8,128)}) async-done(((f32[38400,128]{1,0:T(8,128)}, f32[2880,896]{1,0:T(8,128)}), (f32[38400,128]{1,0:T(8,128)}, f32[2880,896]{1,0:T(8,128)})) %all-reduce.6.cloned.1.call-update) | async-done | bytes 29982736
  (913 shorter events, 570.2 us)
Async XLA Ops:
  7.2 267.9 %copy-start = (bf16[448,896]{1,0:T(8,128)(2,1)S(1)}, bf16[448,896]{1,0:T(8,128)(2,1)}, u32[]{:S(2)}) copy-start(bf16[448,896]{1,0:T(8,128)(2,1)} %param.26) | copy-start | bytes 2408452
  7.2 9.8 copy-start.32
  7.2 9.8 copy-start.54
  7.2 11.1 copy-start.24
  7.2 15.3 %copy-start.14 = (bf16[896,448]{0,1:T(8,128)(2,1)S(1)}, bf16[896,448]{0,1:T(8,128)(2,1)}, u32[]{:S(2)}) copy-start(bf16[896,448]{0,1:T(8,128)(2,1)} %param.20) | copy-start | bytes 2408452
  7.2 15.3 %copy-start.53 = (f32[448]{0:T(512)S(1)}, f32[448]{0:T(512)}, u32[]{:S(2)}) copy-start(f32[448]{0:T(512)} %param.21) | copy-start | bytes 5380
  10.7 5.0 all-to-all-start
  14.2 77.4 %all-gather.2.cloned.1.call-start = ((), (), s32[]{:S(2)}) async-start(), calls=%async_computation.12 | async-start | bytes 5324800 | tf_op jit(solution)/shard_map/all_gather | solution.py:23
  14.3 11.2 copy-start.50
  14.3 11.2 copy-start.44
  19.0 5.0 all-to-all-start.4
  25.7 77.3 %copy-start.35 = (f32[160,32]{0,1:T(8,128)}, f32[160,32]{0,1:T(8,128)S(1)}, u32[]{:S(2)}) copy-start(f32[160,32]{0,1:T(8,128)S(1)} %get-tuple-element.533) | copy-start | bytes 61444
  25.7 77.3 %copy-start.37 = (f32[160,32]{0,1:T(8,128)}, f32[160,32]{0,1:T(8,128)S(1)}, u32[]{:S(2)}) copy-start(f32[160,32]{0,1:T(8,128)S(1)} %get-tuple-element.534) | copy-start | bytes 61444
  279.6 24.0 %copy-start.46 = (f32[2,40]{1,0:T(2,128)}, f32[2,40]{1,0:T(2,128)S(1)}, u32[]{:S(2)}) copy-start(f32[2,40]{1,0:T(2,128)S(1)} %get-tuple-element.537) | copy-start | bytes 964
  279.7 11.6 %slice-start.7 = ((s8[4358144]{0:T(1024)(128)(4,1)}), s8[4194304]{0:T(1024)(128)(4,1)S(1)}, s32[]{:S(2)}) async-start(s8[4358144]{0:T(1024)(128)(4,1)} %bitcast.385), calls=%async_computation.21 | async-start | bytes 8388608
  297.7 5.0 all-to-all-start.5
  666.4 86.2 %all-to-all-start.7 = ((f32[16,4,160,128]{3,2,1,0:T(8,128)}), f32[16,4,160,128]{3,2,1,0:T(8,128)}, u32[]{:S(2)}, u32[]{:S(2)}) async-start(f32[16,4,160,128]{3,2,1,0:T(8,128)} %copy.185), calls=%async_computation.7 | async-start | bytes 10485760 | tf_op jit(solution)/shard_map/all_to_all | solution.py:59
  682.2 9.9 copy-start.13
  682.2 10.0 copy-start.21
  703.9 55.8 %copy-start.17 = (bf16[160,2432]{1,0:T(8,128)(2,1)S(1)}, bf16[160,2432]{1,0:T(8,128)(2,1)}, u32[]{:S(2)}) copy-start(bf16[160,2432]{1,0:T(8,128)(2,1)} %copy-done.16) | copy-start | bytes 2334724
  756.1 18.2 %all-to-all-start.8 = ((f32[4,160,128]{2,1,0:T(8,128)}), f32[4,160,128]{2,1,0:T(8,128)S(1)}, u32[]{:S(2)}, u32[]{:S(2)}) async-start(f32[4,160,128]{2,1,0:T(8,128)} %reduce_sum.196), calls=%async_computation.8 | async-start | bytes 655360 | tf_op jit(solution)/shard_map/all_to_all | solution.py:67
  759.6 372.6 %all-reduce.6.cloned.1.call-start = ((), (), s32[]{:S(2)}) async-start(), calls=%async_computation.13 | async-start | bytes 59965440
  764.4 10.5 copy-start.45
  764.4 10.5 copy-start.51
  826.7 5.2 all-to-all-start.3
  832.7 33.3 %copy-start.8 = (f32[2,40,896]{2,1,0:T(8,128)S(1)}, f32[2,40,896]{2,1,0:T(8,128)}, u32[]{:S(2)}) copy-start(f32[2,40,896]{2,1,0:T(8,128)} %copy-done.7) | copy-start | bytes 860164
  832.7 33.3 %copy-start.47 = (f32[2,40]{1,0:T(2,128)S(1)}, f32[2,40]{1,0:T(2,128)}, u32[]{:S(2)}) copy-start(f32[2,40]{1,0:T(2,128)} %copy-done.46) | copy-start | bytes 964
  832.7 33.3 %copy-start.49 = (f32[2,40]{1,0:T(2,128)S(1)}, f32[2,40]{1,0:T(2,128)}, u32[]{:S(2)}) copy-start(f32[2,40]{1,0:T(2,128)} %copy-done.48) | copy-start | bytes 964
  832.8 33.3 %copy-start.52 = (f32[2,40]{1,0:T(2,128)S(1)}, f32[2,40]{1,0:T(2,128)}, u32[]{:S(2)}) copy-start(f32[2,40]{1,0:T(2,128)} %get-tuple-element.535) | copy-start | bytes 964
  833.8 5.0 all-to-all-start.9
  839.8 10.5 all-to-all-start.10
  851.1 25.7 %all-to-all-start.11 = ((f32[16,1,2944]{2,1,0:T(1,128)}), f32[16,1,2944]{2,1,0:T(1,128)S(1)}, u32[]{:S(2)}, u32[]{:S(2)}) async-start(f32[16,1,2944]{2,1,0:T(1,128)} %broadcast_in_dim.104), calls=%async_computation.11 | async-start | bytes 376832 | tf_op jit(solution)/shard_map/all_to_all | solution.py:29
  (158 other events, 398.7 us)
Sparse Core Ops, SparseCore 0:
  18.5 73.0 all-gather.1
  820.2 311.8 all-reduce.5
where the time goes:
time: 1170 us; the launch traced here: 1150 us
  waiting for transfers between devices  392 us (34%)
  local copies, waits for them, and re-layouts  365 us (31%)
  matrix products  254 us (22%)
  other arithmetic  63.3 us (5%)
  starting transfers between devices  44.4 us (4%)
  between operations  16.8 us (1%)
  blocking collectives  12.9 us (1%)
    unnamed x3, waiting for transfers between devices  254 us
    dynamic_update_slice x80, local copies, waits for them, and re-layouts, local(): lax.scan(backward_block, start_query, pieces_back)  156 us
    dot_general x40, matrix products, masked_scores(): jnp.einsum('qkgd,skd->kgqs', query_low, key_piece, preferred_element_type...  71.9 us
    all_gather x1, waiting for transfers between devices, side_by_side(): result = lax.all_gather(both, axis, axis=dim, tiled=True)  65.7 us
    all_to_all x1, waiting for transfers between devices, sum_at_owner(): lax.all_to_all(blocks, axis, split_axis=0, concat_axis=0, tiled=True)  48.8 us
    dot_general x20, matrix products, backward_block(): jnp.einsum('kgqs,qkgd->skd', attn_probs.astype(jnp.bfloat16), grad_heads,...  46.6 us
    while x260, local copies, waits for them, and re-layouts  36.7 us
    dot_general x20, matrix products, backward_block(): jnp.einsum('qkgd,skd->kgqs', grad_heads, value_piece, preferred_element_t...  34 us
  transfers between devices with their start and end apart: 11, of which 10 were waited for; matrix products, arithmetic and copies ran while one was open for 5% of the time, Pallas kernels for 0%

commit v1 on v0

v1 whole, which is shorter than its diff:
```python
import functools

import jax
import jax.numpy as jnp
from jax import lax
from jax.experimental import pallas as pl
from jax.experimental.pallas import tpu as pltpu
from jax.sharding import Mesh
from jax.sharding import PartitionSpec as P

HEAD_DIM = 64
HEADS = 7
HALF = HEAD_DIM // 2
WIDE = 2 * HEAD_DIM
LANES = 640
CHUNK = 4
CTX = ("ctx_0", "ctx_1", "ctx_2")
ORDERS = (
    ("ctx_0", "ctx_1", "ctx_2"),
    ("ctx_1", "ctx_2", "ctx_0"),
    ("ctx_2", "ctx_0", "ctx_1"),
)
SIDE = 4
EPS = 1e-06
THETA = 1000000.0
NEG_FILL = -1e30
BF = jnp.bfloat16
F32 = jnp.float32


def columns_of(rows, group, block):
    parts = [
        rows[group * block : (group + 1) * block, h * HEAD_DIM : (h + 1) * HEAD_DIM]
        for h in range(HEADS)
    ]
    parts.append(jnp.zeros((LANES - HEADS * block, HEAD_DIM), rows.dtype))
    return jnp.concatenate(parts, axis=0)


def rows_of(columns, block):
    return jnp.concatenate(
        [columns[h * block : (h + 1) * block] for h in range(HEADS)], axis=1
    )


def slot_of(j, me_ref):
    return ((j // SIDE - me_ref[0]) & (SIDE - 1)) * SIDE + ((j % SIDE - me_ref[1]) & (SIDE - 1))


def causal(me2, late, block, query_row):
    shape = (CHUNK, block, LANES)
    b = lax.broadcasted_iota(jnp.int32, shape, 0).reshape(CHUNK * block, LANES)
    r = lax.broadcasted_iota(jnp.int32, shape, 1).reshape(CHUNK * block, LANES)
    ahead = (((b + me2) & (CHUNK - 1)) - me2) * block
    ahead = -ahead if late else ahead
    return ahead + r <= query_row


def forward_kernel(
    me_ref, q_ref, early_ref, late_ref, cos_ref, sin_ref, row_ref, qt_ref, ot_ref, lse_ref, att_ref
):
    block = q_ref.shape[0] // 2
    keys = CHUNK * block
    chunks = early_ref.shape[0]
    mine = me_ref[0] * SIDE + me_ref[1]
    lane = lax.broadcasted_iota(jnp.int32, (keys, WIDE), 1)
    for g in (0, 1):
        qt = columns_of(q_ref[...], g, block).T
        u, w = qt[:HALF], qt[HALF:]
        cos, sin = cos_ref[g], sin_ref[g]
        turned = jnp.concatenate([u * cos - w * sin, w * cos + u * sin], axis=0)
        qt_ref[g, :HEAD_DIM] = turned.astype(BF) * BF(0.125)
        qt_ref[g, HEAD_DIM:] = jnp.zeros((HEAD_DIM, LANES), BF)

    def step(g, ref, masked, j, carry):
        top, acc = carry
        kv = ref[slot_of(j, me_ref)].reshape(keys, WIDE)
        s = jnp.dot(kv, qt_ref[g], preferred_element_type=F32)
        if masked:
            s = jnp.where(causal(me_ref[2], g == 1, block, row_ref[...]), s, NEG_FILL)
        new = jnp.maximum(top, jnp.max(s, axis=0, keepdims=True))
        p = jnp.exp(s - new).astype(BF)
        shrink = jnp.exp(top - new)
        ones_v = jnp.where(lane < HEAD_DIM, BF(1), kv)
        more = lax.dot_general(ones_v, p, (((0,), (0,)), ((), ())), preferred_element_type=F32)
        return new, acc * shrink + more

    for g in (0, 1):
        carry = (jnp.full((1, LANES), NEG_FILL, F32), jnp.zeros((WIDE, LANES), F32))
        if g == 0:
            carry = lax.fori_loop(
                0, mine, functools.partial(step, 0, early_ref, False), carry
            )
            carry = step(0, early_ref, True, mine, carry)
        else:
            carry = lax.fori_loop(
                0, chunks, functools.partial(step, 1, early_ref, False), carry
            )
            carry = step(1, late_ref, True, mine, carry)
            carry = lax.fori_loop(
                mine + 1, chunks, functools.partial(step, 1, late_ref, False), carry
            )
        top, acc = carry
        total = acc[0:1]
        out = acc[HEAD_DIM:] / total
        ot_ref[g] = out
        lse_ref[g] = top + jnp.log(total)
        att_ref[g * block : (g + 1) * block] = rows_of(out.T, block).astype(BF)


def backward_kernel(
    me_ref,
    qt_ref,
    ot_ref,
    lse_ref,
    grad_ref,
    early_ref,
    late_ref,
    cos_ref,
    sin_ref,
    row_ref,
    dq_ref,
    de_ref,
    dl_ref,
    sum_ref,
):
    block = grad_ref.shape[0] // 2
    keys = CHUNK * block
    chunks = early_ref.shape[0]
    mine = me_ref[0] * SIDE + me_ref[1]

    def clear(j, unused):
        dl_ref[slot_of(j, me_ref)] = jnp.zeros((CHUNK, block, WIDE), dl_ref.dtype)
        return unused

    lax.fori_loop(0, mine, clear, 0)

    for g in (1, 0):
        qt = qt_ref[g]
        grad = columns_of(grad_ref[...].astype(F32), g, block)
        none = jnp.zeros((LANES, HEAD_DIM), F32)
        grad_rows = jnp.concatenate([none, grad], axis=1)
        grad_t = grad_rows.T
        delta = jnp.sum(grad_t[HEAD_DIM:] * ot_ref[g], axis=0, keepdims=True)
        grad_rows = grad_rows.astype(BF)
        grad_t = grad_t.astype(BF)
        q_rows = qt.astype(F32).T.astype(BF)
        lse = lse_ref[g]

        def step(
            early, masked, j, dqt, g=g, qt=qt, rows=grad_rows, cols=grad_t, q=q_rows, lse=lse, d=delta
        ):
            slot = slot_of(j, me_ref)
            kv = (early_ref if early else late_ref)[slot].reshape(keys, WIDE)
            s = jnp.dot(kv, qt, preferred_element_type=F32)
            p = jnp.exp(s - lse)
            if masked:
                p = jnp.where(causal(me_ref[2], g == 1, block, row_ref[...]), p, 0.0)
            dp = jnp.dot(kv, cols, preferred_element_type=F32)
            ds = (p * (dp - d)).astype(BF)
            dkv = jnp.dot(ds, q, preferred_element_type=F32) + jnp.dot(
                p.astype(BF), rows, preferred_element_type=F32
            )
            dqt = dqt + lax.dot_general(
                kv, ds, (((0,), (0,)), ((), ())), preferred_element_type=F32
            )
            if g == 0:
                dkv = dkv + sum_ref[slot].reshape(keys, WIDE)
            dkv = dkv.reshape(CHUNK, block, WIDE)
            if not early:
                dl_ref[slot] = dkv.astype(dl_ref.dtype)
            elif g == 0:
                de_ref[slot] = dkv.astype(de_ref.dtype)
            else:
                sum_ref[slot] = dkv
            return dqt

        dqt = jnp.zeros((WIDE, LANES), F32)
        if g == 1:
            dqt = lax.fori_loop(0, chunks, functools.partial(step, True, False), dqt)
            dqt = step(False, True, mine, dqt)
            dqt = lax.fori_loop(mine + 1, chunks, functools.partial(step, False, False), dqt)
        else:
            dqt = lax.fori_loop(0, mine, functools.partial(step, True, False), dqt)
            dqt = step(True, True, mine, dqt)
        u, w = dqt[:HALF] * 0.125, dqt[HALF:HEAD_DIM] * 0.125
        cos, sin = cos_ref[g], sin_ref[g]
        dq = jnp.concatenate([u * cos + w * sin, w * cos - u * sin], axis=0).T
        dq_ref[g * block : (g + 1) * block] = rows_of(dq, block).astype(dq_ref.dtype)

    def finish(j, unused):
        slot = slot_of(j, me_ref)
        de_ref[slot] = sum_ref[slot].astype(de_ref.dtype)
        return unused

    lax.fori_loop(mine + 1, chunks, finish, 0)


VMEM = pl.BlockSpec(memory_space=pltpu.VMEM)
SMEM = pl.BlockSpec(memory_space=pltpu.SMEM)
PARAMS = pltpu.CompilerParams(vmem_limit_bytes=40 * 1024 * 1024)


def attend(me, q, early, late, cos, sin, rows):
    own = q.shape[0]
    return pl.pallas_call(
        forward_kernel,
        out_shape=(
            jax.ShapeDtypeStruct((2, WIDE, LANES), BF),
            jax.ShapeDtypeStruct((2, HEAD_DIM, LANES), F32),
            jax.ShapeDtypeStruct((2, 1, LANES), F32),
            jax.ShapeDtypeStruct((own, HEADS * HEAD_DIM), BF),
        ),
        in_specs=[SMEM] + [VMEM] * 6,
        out_specs=(VMEM,) * 4,
        compiler_params=PARAMS,
        cost_estimate=pl.CostEstimate(
            flops=22_000_000_000, bytes_accessed=4_000_000, transcendentals=0
        ),
        name="attend",
    )(me, q, early, late, cos, sin, rows)


def attend_back(me, qt, ot, lse, grad, early, late, cos, sin, rows):
    own = grad.shape[0]
    return pl.pallas_call(
        backward_kernel,
        out_shape=(
            jax.ShapeDtypeStruct((own, HEADS * HEAD_DIM), BF),
            jax.ShapeDtypeStruct(early.shape, BF),
            jax.ShapeDtypeStruct(late.shape, BF),
        ),
        in_specs=[SMEM] + [VMEM] * 9,
        out_specs=(VMEM,) * 3,
        scratch_shapes=[pltpu.VMEM(early.shape, F32)],
        compiler_params=PARAMS,
        cost_estimate=pl.CostEstimate(
            flops=28_000_000_000, bytes_accessed=8_000_000, transcendentals=0
        ),
        name="attend_back",
    )(me, qt, ot, lse, grad, early, late, cos, sin, rows)


def send(array, axis, s):
    return lax.ppermute(array, axis, [(i, (i + s) % SIDE) for i in range(SIDE)])


def fetch(array, axis, s):
    return lax.ppermute(array, axis, [(i, (i - s) % SIDE) for i in range(SIDE)])


def other_core(array):
    return lax.ppermute(array, "tp", [(0, 1), (1, 0)])


def gather(array, axis, dim):
    return jnp.stack([array] + [fetch(array, axis, s) for s in range(1, SIDE)], axis=dim)


def total_of(arrays):
    total = arrays[0].astype(F32)
    for a in arrays[1:]:
        total = total + a.astype(F32)
    return total


def sum_at_owner(pieces, axes):
    for axis in axes[:-1]:
        arrays = [pieces[0]] + [send(pieces[s], axis, s) for s in range(1, SIDE)]
        rows = arrays[0].shape[0] // SIDE
        pieces = [
            total_of([a[s * rows : (s + 1) * rows] for a in arrays]).astype(BF)
            for s in range(SIDE)
        ]
    return total_of([pieces[0]] + [send(pieces[s], axes[-1], s) for s in range(1, SIDE)])


def sum_everywhere(vector):
    for axis in CTX:
        vector = total_of([vector] + [fetch(vector, axis, s) for s in range(1, SIDE)])
    return vector + other_core(vector)


def by_distance(me, order, width):
    each = width // SIDE**3
    place = jnp.arange(width)
    part, within = place // each, place % each
    apart = dict(zip(order, (part // SIDE**2, part // SIDE % SIDE, part % SIDE)))
    d0, d1, d2 = [(me[k] + apart[a]) % SIDE for k, a in enumerate(CTX)]
    feature = ((d0 * SIDE + d1) * SIDE + d2) * each + within
    return (jnp.arange(width)[:, None] == feature[None, :]).astype(BF)


def rearranged(rows, table):
    return jnp.dot(rows, table, preferred_element_type=F32).astype(BF)


def weight_pieces(rows, grads):
    size = rows.shape[1] // SIDE
    return [
        lax.dot_general(
            rows[:, s * size : (s + 1) * size],
            grads,
            (((0,), (0,)), ((), ())),
            preferred_element_type=F32,
        ).astype(BF)
        for s in range(SIDE)
    ]


def rms_forward(rows, gain):
    inverse = lax.rsqrt(jnp.mean(rows * rows, axis=-1, keepdims=True) + EPS)
    return (rows * inverse * gain, inverse)


def rms_backward(rows, inverse, gain, grad_out):
    weighted = grad_out * gain
    inner = jnp.mean(rows * weighted, axis=-1, keepdims=True)
    return inverse * weighted - rows * (inverse * inverse * inverse) * inner


def angles(positions):
    freqs = 1.0 / THETA ** (jnp.arange(0, HEAD_DIM, 2).astype(F32) / HEAD_DIM)
    return positions.astype(F32), freqs


def local(
    tokens,
    gain_attn,
    query_projection_weight,
    query_bias_vector,
    key_projection_weight,
    key_bias_vector,
    value_projection_weight,
    value_bias_vector,
    w_output,
    gain_mlp,
    w_gate,
    w_up,
    w_down,
    cotangent,
):
    me = [lax.axis_index(a) for a in CTX]
    tp = lax.axis_index("tp")
    ctx_count = SIDE**3
    ctx = (me[0] * SIDE + me[1]) * SIDE + me[2]
    half = tokens.shape[2]
    block = 2 * half
    width = tokens.shape[3]
    own = 2 * block
    places = jnp.stack([me[0], me[1], me[2], tp]).astype(jnp.int32)

    def both_halves(array):
        parts = lax.all_gather(array.reshape(2, half, width), "tp", axis=0)
        return jnp.moveaxis(parts, 0, 1).reshape(own, width)

    def own_half(array):
        return lax.dynamic_index_in_dim(
            array.reshape(2, 2, half, width), tp, 1, keepdims=False
        ).reshape(block, width)

    def other_half(array):
        return lax.dynamic_index_in_dim(
            array.reshape(2, 2, half, width), 1 - tp, 1, keepdims=False
        ).reshape(block, width)

    firsts = jnp.stack([ctx * block, (2 * ctx_count - 1 - ctx) * block])
    row = jnp.arange(LANES) % block
    row = jnp.where(jnp.arange(LANES) < HEADS * block, row, 0)
    lane_places, freqs = angles(firsts[:, None] + row[None, :])
    lane_angles = lane_places[:, None, :] * freqs[None, :, None]
    lane_cos, lane_sin = jnp.cos(lane_angles), jnp.sin(lane_angles)
    own_places, freqs = angles((firsts[:, None] + jnp.arange(block)[None, :]).reshape(-1))
    own_angles = own_places[:, None] * freqs[None, :]
    cos, sin = jnp.cos(own_angles), jnp.sin(own_angles)
    query_row = row.astype(jnp.int32)[None, :]

    x_all = both_halves(tokens).astype(F32)
    n1, inverse_attn = rms_forward(x_all, gain_attn)
    n1 = n1.astype(BF)
    key_pre = jnp.dot(n1, key_projection_weight, preferred_element_type=F32) + key_bias_vector
    value_pre = jnp.dot(n1, value_projection_weight, preferred_element_type=F32) + value_bias_vector
    u, w = key_pre[:, :HALF], key_pre[:, HALF:]
    kv_own = jnp.concatenate([u * cos - w * sin, w * cos + u * sin, value_pre], axis=1)
    kv_own = kv_own.astype(BF).reshape(2, block, WIDE)
    kv_row = gather(kv_own, "ctx_2", 1)
    early = gather(gather(kv_row[0], "ctx_1", 0), "ctx_0", 0)
    late = gather(gather(kv_row[1], "ctx_0", 0), "ctx_1", 1)
    shape = (SIDE * SIDE, CHUNK, block, WIDE)
    early, late = early.reshape(shape), late.reshape(shape)

    query_pre = (
        jnp.dot(n1, query_projection_weight, preferred_element_type=F32) + query_bias_vector
    )
    dy_all = both_halves(cotangent)
    tables = [by_distance(me, order, width) for order in ORDERS]
    grad_act = jnp.einsum("rd,fd->rf", dy_all, w_down, preferred_element_type=F32)
    dy_2 = rearranged(dy_all, tables[2])
    n1_1 = rearranged(n1, tables[1])
    n1_0 = rearranged(n1, tables[0])

    qt, ot, lse, attended = attend(places, query_pre, early, late, lane_cos, lane_sin, query_row)
    attn_term = jnp.dot(attended, w_output, preferred_element_type=F32).astype(BF)
    attn_rows = attn_term.astype(F32) + other_core(attn_term).astype(F32)
    hidden = x_all + attn_rows

    n2, inverse_mlp = rms_forward(hidden, gain_mlp)
    n2 = n2.astype(BF)
    gate_rows = jnp.dot(n2, w_gate, preferred_element_type=F32)
    up_rows = jnp.dot(n2, w_up, preferred_element_type=F32)
    sigmoid_gate = jax.nn.sigmoid(gate_rows)
    silu_gate = gate_rows * sigmoid_gate
    activation = (silu_gate * up_rows).astype(BF)
    grad_gate = (
        grad_act * up_rows * sigmoid_gate * (1.0 + gate_rows * (1.0 - sigmoid_gate))
    ).astype(BF)
    grad_up = (grad_act * silu_gate).astype(BF)
    down_pieces = weight_pieces(dy_2, activation)
    gate_pieces = weight_pieces(rearranged(n2, tables[0]), grad_gate)
    up_pieces = weight_pieces(rearranged(n2, tables[1]), grad_up)
    dn2_term = (
        jnp.einsum("rf,df->rd", grad_gate, w_gate, preferred_element_type=F32)
        + jnp.einsum("rf,df->rd", grad_up, w_up, preferred_element_type=F32)
    ).astype(BF)
    dn2 = dn2_term.astype(F32) + other_core(dn2_term).astype(F32)
    mlp_term = jnp.dot(activation, w_down, preferred_element_type=F32).astype(BF)
    mlp_rows = own_half(mlp_term).astype(F32) + other_core(other_half(mlp_term)).astype(F32)
    mixed = (own_half(hidden) + mlp_rows).astype(BF).reshape(tokens.shape)

    grad_hidden = dy_all.astype(F32) + rms_backward(hidden, inverse_mlp, gain_mlp, dn2)
    grad_gain_mlp = jnp.sum(dn2 * hidden * inverse_mlp, axis=0)
    grad_attn = grad_hidden.astype(BF)
    grad_attended = jnp.einsum(
        "rd,qd->rq", grad_attn, w_output, preferred_element_type=F32
    ).astype(BF)
    output_pieces = weight_pieces(rearranged(grad_attn, tables[2]), attended)
    gate_shard = sum_at_owner(gate_pieces, ORDERS[0])
    up_shard = sum_at_owner(up_pieces, ORDERS[1])
    down_shard = sum_at_owner(down_pieces, ORDERS[2]).T
    output_shard = sum_at_owner(output_pieces, ORDERS[2]).T

    grad_query, grad_early, grad_late = attend_back(
        places, qt, ot, lse, grad_attended, early, late, lane_cos, lane_sin, query_row
    )
    cube = (SIDE, SIDE, CHUNK, block, WIDE)
    flat = (SIDE * CHUNK, block, WIDE)
    grad_early, grad_late = grad_early.reshape(cube), grad_late.reshape(cube)
    own_early = sum_at_owner([grad_early[s].reshape(flat) for s in range(SIDE)], CTX)
    own_late = sum_at_owner(
        [grad_late[:, s].reshape(flat) for s in range(SIDE)], ("ctx_1", "ctx_0", "ctx_2")
    )
    grad_kv = jnp.concatenate([own_early, own_late], axis=0).reshape(own, WIDE)
    u, w = grad_kv[:, :HALF], grad_kv[:, HALF:HEAD_DIM]
    grad_kv = jnp.concatenate(
        [u * cos + w * sin, w * cos - u * sin, grad_kv[:, HEAD_DIM:]], axis=1
    ).astype(BF)

    query_shard = sum_at_owner(weight_pieces(n1_1, grad_query), ORDERS[1])
    kv_shard = sum_at_owner(weight_pieces(n1_0, grad_kv), ORDERS[0])
    dn1_term = jnp.einsum(
        "rq,dq->rd", grad_query, query_projection_weight, preferred_element_type=F32
    )
    kv_weight = jnp.concatenate([key_projection_weight, value_projection_weight], axis=1)
    dn1_term = dn1_term + jnp.einsum("rq,dq->rd", grad_kv, kv_weight, preferred_element_type=F32)
    grad_gain_attn = jnp.sum(dn1_term * x_all * inverse_attn, axis=0)
    dn1_term = dn1_term.astype(BF)
    dn1 = own_half(dn1_term).astype(F32) + other_core(other_half(dn1_term)).astype(F32)
    x_own = tokens.astype(F32).reshape(block, width)
    inverse_own = lax.rsqrt(jnp.mean(x_own * x_own, axis=-1, keepdims=True) + EPS)
    grad_tokens = own_half(grad_hidden) + rms_backward(x_own, inverse_own, gain_attn, dn1)
    grad_tokens = grad_tokens.astype(BF).reshape(tokens.shape)

    first = tp == 0

    def both_cores(vector):
        none = jnp.zeros_like(vector)
        return jnp.concatenate([jnp.where(first, vector, none), jnp.where(first, none, vector)])

    kv_sums = jnp.sum(grad_kv.astype(F32), axis=0)
    vectors = (
        grad_gain_attn,
        jnp.where(first, grad_gain_mlp, 0.0),
        both_cores(jnp.sum(grad_query.astype(F32), axis=0)),
        both_cores(kv_sums[:HEAD_DIM]),
        both_cores(kv_sums[HEAD_DIM:]),
    )
    sizes = [v.shape[0] for v in vectors]
    packed = jnp.concatenate(vectors).reshape(-1, 128)
    sums = jnp.split(sum_everywhere(packed).reshape(-1), [sum(sizes[:k]) for k in range(1, 5)])
    return (
        mixed,
        grad_tokens,
        sums[0],
        query_shard,
        sums[2],
        kv_shard[:, :HEAD_DIM],
        sums[3],
        kv_shard[:, HEAD_DIM:],
        sums[4],
        output_shard,
        sums[1],
        gate_shard,
        up_shard,
        down_shard,
    )


def solution(mesh):
    split = Mesh(mesh.devices.reshape(SIDE, SIDE, SIDE, mesh.shape["tp"]), (*CTX, "tp"))
    return jax.shard_map(
        local,
        mesh=split,
        in_specs=(
            P(CTX, None, "tp", None),
            P(),
            P(None, "tp"),
            P("tp"),
            P(None, "tp"),
            P("tp"),
            P(None, "tp"),
            P("tp"),
            P("tp", None),
            P(),
            P(None, "tp"),
            P(None, "tp"),
            P("tp", None),
            P(CTX, None, "tp", None),
        ),
        out_specs=(
            P(CTX, None, "tp", None),
            P(CTX, None, "tp", None),
            P(),
            P(CTX, "tp"),
            P(),
            P(CTX, "tp"),
            P(),
            P(CTX, "tp"),
            P(),
            P("tp", CTX),
            P(),
            P(CTX, "tp"),
            P(CTX, "tp"),
            P("tp", CTX),
        ),
        check_vma=False,
    )
```

time: 1170 us -> 443 us (0.38); the launches traced: 1150 us -> 439 us
  local copies, waits for them, and re-layouts: 365 us -> 6.65 us
  waiting for transfers between devices: 392 us -> 167 us
  matrix products: 254 us -> 43.2 us
  starting transfers between devices: 44.4 us -> 155 us
  other arithmetic: 63.3 us -> 15 us
  Pallas kernels: 0 us -> 45.3 us
  between operations: 16.8 us -> 2.09 us
    unnamed x3 -> x0, waiting for transfers between devices: 254 us -> none
    dot_general x161 -> x43, matrix products: 254 us -> 43.2 us  [the longest x24 22.1 us: weight_pieces(): lax.dot_general(rows[:, s * size:(s + 1) * size], grads, (((0,), (0,)), (...]
    ppermute x0 -> x101, waiting for transfers between devices: none -> 167 us  [the longest x72 141 us: send(): return lax.ppermute(array, axis, [(i, (i + s) % SIDE) for i in range(SIDE)])]
    dynamic_update_slice x83 -> x0, local copies, waits for them, and re-layouts: 157 us -> none  [the longest x80 156 us: local(): lax.scan(backward_block, start_query, pieces_back)]
    ppermute x0 -> x101, starting transfers between devices: none -> 155 us  [the longest x72 104 us: send(): return lax.ppermute(array, axis, [(i, (i + s) % SIDE) for i in range(SIDE)])]
    all_to_all x9 -> x0, waiting for transfers between devices: 71.7 us -> none  [the longest x1 48.8 us: sum_at_owner(): lax.all_to_all(blocks, axis, split_axis=0, concat_axis=0, tiled=True)]
    all_gather x1 -> x0, waiting for transfers between devices: 65.7 us -> none  [side_by_side(): result = lax.all_gather(both, axis, axis=dim, tiled=True)]
    pallas_call x0 -> x2, Pallas kernels: none -> 45.3 us  [the longest x1 24.3 us: attend_back(): pl.pallas_call(backward_kernel, out_shape=(jax.ShapeDtypeStruct((own, HEA...]
  transfers between devices with their start and end apart: 11 -> 101, of which waited for: 10 -> 40; matrix products, arithmetic and copies ran while one was open for 5% -> 6% of each run, Pallas kernels for 0% -> 0%
where the time goes in v1:
time: 443 us; the launch traced here: 439 us
  waiting for transfers between devices  167 us (38%)
  starting transfers between devices  155 us (35%)
  Pallas kernels  45.3 us (10%)
  matrix products  43.2 us (10%)
  other arithmetic  15 us (3%)
  local copies, waits for them, and re-layouts  6.65 us (2%)
    ppermute x72, waiting for transfers between devices, send(): return lax.ppermute(array, axis, [(i, (i + s) % SIDE) for i in range(SIDE)])  141 us
    ppermute x72, starting transfers between devices, send(): return lax.ppermute(array, axis, [(i, (i + s) % SIDE) for i in range(SIDE)])  104 us
    ppermute x24, starting transfers between devices, fetch(): return lax.ppermute(array, axis, [(i, (i - s) % SIDE) for i in range(SIDE)])  41.5 us
    pallas_call x1, Pallas kernels, attend_back(): pl.pallas_call(backward_kernel, out_shape=(jax.ShapeDtypeStruct((own, HEA...  24.3 us
    ppermute x24, waiting for transfers between devices, fetch(): return lax.ppermute(array, axis, [(i, (i - s) % SIDE) for i in range(SIDE)])  22.9 us
    dot_general x24, matrix products, weight_pieces(): lax.dot_general(rows[:, s * size:(s + 1) * size], grads, (((0,), (0,)), (...  22.1 us
    pallas_call x1, Pallas kernels, attend(): pl.pallas_call(forward_kernel, out_shape=(jax.ShapeDtypeStruct((2, WIDE,...  21 us
    ppermute x5, starting transfers between devices, other_core(): return lax.ppermute(array, 'tp', [(0, 1), (1, 0)])  9.66 us
  transfers between devices with their start and end apart: 101, of which 40 were waited for; matrix products, arithmetic and copies ran while one was open for 6% of the time, Pallas kernels for 0%

profile of v1, /device:TPU:0, one launch (start us, length us, event | category | flops | bytes accessed | tf_op | source)
XLA Modules:
  0.0 438.9 jit_solution(5746990575890912512)
XLA Ops:
  7.4 3.6 collective-permute-start.1
  38.0 4.6 %collective-permute-done.11 = bf16[4,80,128]{2,1,0:T(8,128)(2,1)S(1)} collective-permute-done((bf16[4,80,128]{2,1,0:T(8,128)(2,1)S(1)}, bf16[4,80,128]{2,1,0:T(8,128)(2,1)S(1)}, u32[]{:S(2)}, u32[]{:S(2)}) %collective-permute-start.11) | collective-permute-done | bytes 81952 | tf_op jit(solution)/shard_map/ppermute | solution.py:249
  42.5 2.9 collective-permute-start.6
  47.9 3.0 collective-permute-start.13
  53.1 7.6 %collective-permute-done.14 = bf16[4,4,80,128]{3,2,1,0:T(8,128)(2,1)S(1)} collective-permute-done((bf16[4,4,80,128]{3,2,1,0:T(8,128)(2,1)S(1)}, bf16[4,4,80,128]{3,2,1,0:T(8,128)(2,1)S(1)}, u32[]{:S(2)}, u32[]{:S(2)}) %collective-permute-start.14) | collective-permute-done | bytes 327712 | tf_op jit(solution)/shard_map/ppermute | solution.py:249
  61.4 21.0 %attend.1 = (bf16[2,128,640]{2,1,0:T(8,128)(2,1)S(1)}, f32[2,64,640]{2,1,0:T(8,128)S(1)}, f32[2,1,640]{2,1,0:T(1,128)S(1)}, bf16[160,448]{1,0:T(8,128)(2,1)S(1)}) custom-call(s32[4]{0:T(128)S(1)} %pad_add_fusion.me_ref, f32[160,448]{1,0:T(8,128)S(1)} %convolution_add_fusion.2.q_ref, bf16[16,4,80,128]{3,2,1,0:T(8,128)(2,1)S(1)} %bitcast.209, ...), custom_call_target="tpu_custom_call" | custom-call | flops 22000001024 | bytes 4000000 | tf_op jit(solution)/shard_map/attend/pallas_call | solution.py:206
  87.8 3.4 fusion.156
  115.1 9.3 %collective-permute-start.17 = (bf16[160,896]{1,0:T(8,128)(2,1)S(1)}, bf16[160,896]{1,0:T(8,128)(2,1)S(1)}, u32[]{:S(2)}, u32[]{:S(2)}) collective-permute-start(bf16[160,896]{1,0:T(8,128)(2,1)S(1)} %fusion.13), channel_id=1, source_target_pairs={{0,1},{1,0},{2,3},{3,2},{4,5},{5,4},{6,7},{7,6},{8,9},{9,8},{10,11... | collective-permute-start | bytes 860168 | tf_op jit(solution)/shard_map/ppermute | solution.py:253
  128.3 24.3 %attend_back.1 = (bf16[160,448]{1,0:T(8,128)(2,1)S(1)}, bf16[16,4,80,128]{3,2,1,0:T(8,128)(2,1)S(1)}, bf16[16,4,80,128]{3,2,1,0:T(8,128)(2,1)S(1)}) custom-call(s32[4]{0:T(128)S(1)} %pad_add_fusion.me_ref, bf16[2,128,640]{2,1,0:T(8,128)(2,1)S(1)} %get-tuple-element.22.qt_ref, f32[2,64,640]{2,1,0:T(8,128)S(1)} %copy-done.5, ...), custom_call_target="tpu_custom_call" | custom-call | flops 28000000000 | bytes 8000000 | tf_op jit(solution)/shard_map/attend_back/pallas_call | solution.py:226
  162.1 14.5 %collective-permute-done.49 = bf16[224,448]{1,0:T(8,128)(2,1)S(1)} collective-permute-done((bf16[224,448]{1,0:T(8,128)(2,1)S(1)}, bf16[224,448]{1,0:T(8,128)(2,1)S(1)}, u32[]{:S(2)}, u32[]{:S(2)}) %collective-permute-start.49) | collective-permute-done | bytes 200736 | tf_op jit(solution)/shard_map/ppermute | solution.py:245
  177.6 2.9 collective-permute-start.52
  187.9 4.6 %collective-permute-start.70 = (bf16[56,448]{1,0:T(8,128)(2,1)S(1)}, bf16[56,448]{1,0:T(8,128)(2,1)S(1)}, u32[]{:S(2)}, u32[]{:S(2)}) collective-permute-start(bf16[56,448]{1,0:T(8,128)(2,1)S(1)} %get-tuple-element.71), channel_id=1, source_target_pairs={{0,96},{32,0},{64,32},{96,64},{1,97},{33,1},{65,33},{97,65},{2,98}... | collective-permute-start | bytes 150536 | tf_op jit(solution)/shard_map/ppermute | solution.py:245
  199.5 6.4 %collective-permute-start.73 = (bf16[14,448]{1,0:T(8,128)(2,1)S(1)}, bf16[14,448]{1,0:T(8,128)(2,1)S(1)}, u32[]{:S(2)}, u32[]{:S(2)}) collective-permute-start(bf16[14,448]{1,0:T(8,128)(2,1)S(1)} %get-tuple-element.95), channel_id=1, source_target_pairs={{0,24},{8,0},{16,8},{24,16},{1,25},{9,1},{17,9},{25,17},{2,26},{10... | collective-permute-start | bytes 37640 | tf_op jit(solution)/shard_map/ppermute | solution.py:245
  211.3 11.6 %collective-permute-done.72 = bf16[14,448]{1,0:T(8,128)(2,1)S(1)} collective-permute-done((bf16[14,448]{1,0:T(8,128)(2,1)S(1)}, bf16[14,448]{1,0:T(8,128)(2,1)S(1)}, u32[]{:S(2)}, u32[]{:S(2)}) %collective-permute-start.72) | collective-permute-done | bytes 12576 | tf_op jit(solution)/shard_map/ppermute | solution.py:245
  230.6 6.9 %collective-permute-done.20 = bf16[16,80,128]{2,1,0:T(8,128)(2,1)S(1)} collective-permute-done((bf16[16,80,128]{2,1,0:T(8,128)(2,1)S(1)}, bf16[16,80,128]{2,1,0:T(8,128)(2,1)S(1)}, u32[]{:S(2)}, u32[]{:S(2)}) %collective-permute-start.20) | collective-permute-done | bytes 327712 | tf_op jit(solution)/shard_map/ppermute | solution.py:245
  237.7 4.8 %collective-permute-start.30 = (bf16[4,80,128]{2,1,0:T(8,128)(2,1)S(1)}, bf16[4,80,128]{2,1,0:T(8,128)(2,1)S(1)}, u32[]{:S(2)}, u32[]{:S(2)}) collective-permute-start(bf16[4,80,128]{2,1,0:T(8,128)(2,1)S(1)} %get-tuple-element.54), channel_id=1, source_target_pairs={{0,32},{32,64},{64,96},{96,0},{1,33},{33,65},{65,97},{97,1},{2,34}... | collective-permute-start | bytes 245768 | tf_op jit(solution)/shard_map/ppermute | solution.py:245
  242.8 20.0 %collective-permute-done.32 = bf16[4,80,128]{2,1,0:T(8,128)(2,1)S(1)} collective-permute-done((bf16[4,80,128]{2,1,0:T(8,128)(2,1)S(1)}, bf16[4,80,128]{2,1,0:T(8,128)(2,1)S(1)}, u32[]{:S(2)}, u32[]{:S(2)}) %collective-permute-start.32) | collective-permute-done | bytes 81952 | tf_op jit(solution)/shard_map/ppermute | solution.py:245
  264.0 4.8 %collective-permute-done.22 = bf16[4,80,128]{2,1,0:T(8,128)(2,1)S(1)} collective-permute-done((bf16[4,80,128]{2,1,0:T(8,128)(2,1)S(1)}, bf16[4,80,128]{2,1,0:T(8,128)(2,1)S(1)}, u32[]{:S(2)}, u32[]{:S(2)}) %collective-permute-start.22) | collective-permute-done | bytes 81952 | tf_op jit(solution)/shard_map/ppermute | solution.py:245
  273.8 3.6 collective-permute-done.25
  279.4 4.6 %collective-permute-start.38 = (f32[23,128]{1,0:T(8,128)S(1)}, f32[23,128]{1,0:T(8,128)S(1)}, u32[]{:S(2)}, u32[]{:S(2)}) collective-permute-start(f32[23,128]{1,0:T(8,128)S(1)} %bitcast.259), channel_id=1, source_target_pairs={{0,64},{32,96},{64,0},{96,32},{1,65},{33,97},{65,1},{97,33},{2,66}... | collective-permute-start | bytes 35336 | tf_op jit(solution)/shard_map/ppermute | solution.py:249
  302.9 3.2 collective-permute-start.75
  310.8 3.3 collective-permute-done.60
  328.4 3.1 collective-permute-done.75
  333.1 21.0 %collective-permute-done.74 = bf16[224,2432]{1,0:T(8,128)(2,1)S(1)} collective-permute-done((bf16[224,2432]{1,0:T(8,128)(2,1)}, bf16[224,2432]{1,0:T(8,128)(2,1)S(1)}, u32[]{:S(2)}, u32[]{:S(2)}) %collective-permute-start.74) | collective-permute-done | bytes 1089568 | tf_op jit(solution)/shard_map/ppermute | solution.py:245
  358.2 15.0 %collective-permute-start.79 = (bf16[56,2432]{1,0:T(8,128)(2,1)S(1)}, bf16[56,2432]{1,0:T(8,128)(2,1)S(1)}, u32[]{:S(2)}, u32[]{:S(2)}) collective-permute-start(bf16[56,2432]{1,0:T(8,128)(2,1)S(1)} %get-tuple-element.41), channel_id=1, source_target_pairs={{0,24},{8,0},{16,8},{24,16},{1,25},{9,1},{17,9},{25,17},{2,26},{10... | collective-permute-start | bytes 817160 | tf_op jit(solution)/shard_map/ppermute | solution.py:245
  373.2 2.9 collective-permute-done.83
  378.2 4.3 collective-permute-done.93
  383.1 21.8 %collective-permute-done.92 = bf16[224,2432]{1,0:T(8,128)(2,1)S(1)} collective-permute-done((bf16[224,2432]{1,0:T(8,128)(2,1)S(1)}, bf16[224,2432]{1,0:T(8,128)(2,1)S(1)}, u32[]{:S(2)}, u32[]{:S(2)}) %collective-permute-start.92) | collective-permute-done | bytes 1089568 | tf_op jit(solution)/shard_map/ppermute | solution.py:245
  407.4 3.2 collective-permute-start.96
  412.3 3.6 collective-permute-done.87
  415.9 4.9 %collective-permute-done.86 = bf16[56,2432]{1,0:T(8,128)(2,1)S(1)} collective-permute-done((bf16[56,2432]{1,0:T(8,128)(2,1)S(1)}, bf16[56,2432]{1,0:T(8,128)(2,1)S(1)}, u32[]{:S(2)}, u32[]{:S(2)}) %collective-permute-start.86) | collective-permute-done | bytes 272416 | tf_op jit(solution)/shard_map/ppermute | solution.py:245
  433.4 3.2 collective-permute-done.99
  (403 shorter events, 183.0 us)
Async XLA Ops:
  5.4 15.6 %collective-permute-start.2 = (bf16[2,80,128]{2,1,0:T(8,128)(2,1)S(1)}, bf16[2,80,128]{2,1,0:T(8,128)(2,1)S(1)}, u32[]{:S(2)}, u32[]{:S(2)}) collective-permute-start(bf16[2,80,128]{2,1,0:T(8,128)(2,1)S(1)} %pad_maximum_fusion.6), channel_id=1, source_target_pairs={{0,2},{2,4},{4,6},{6,0},{1,3},{3,5},{5,7},{7,1},{8,10},{10,12},{12... | collective-permute-start | bytes 122888 | tf_op jit(solution)/shard_map/ppermute | solution.py:249
  30.0 20.9 %collective-permute-start.8 = (bf16[4,4,80,128]{3,2,1,0:T(8,128)(2,1)S(1)}, bf16[4,4,80,128]{3,2,1,0:T(8,128)(2,1)S(1)}, u32[]{:S(2)}, u32[]{:S(2)}) collective-permute-start(bf16[4,4,80,128]{3,2,1,0:T(8,128)(2,1)S(1)} %get-tuple-element.89), channel_id=1, source_target_pairs={{0,32},{32,64},{64,96},{96,0},{1,33},{33,65},{65,97},{97,1},{2,34}... | collective-permute-start | bytes 983048 | tf_op jit(solution)/shard_map/ppermute | solution.py:249
  37.3 15.0 %collective-permute-start.7 = (bf16[4,4,80,128]{3,2,1,0:T(8,128)(2,1)S(1)}, bf16[4,4,80,128]{3,2,1,0:T(8,128)(2,1)S(1)}, u32[]{:S(2)}, u32[]{:S(2)}) collective-permute-start(bf16[4,4,80,128]{3,2,1,0:T(8,128)(2,1)S(1)} %get-tuple-element.89), channel_id=1, source_target_pairs={{0,64},{32,96},{64,0},{96,32},{1,65},{33,97},{65,1},{97,33},{2,66}... | collective-permute-start | bytes 983048 | tf_op jit(solution)/shard_map/ppermute | solution.py:249
  156.9 68.5 %collective-permute-start.29 = (bf16[16,80,128]{2,1,0:T(8,128)(2,1)S(1)}, bf16[16,80,128]{2,1,0:T(8,128)(2,1)S(1)}, u32[]{:S(2)}, u32[]{:S(2)}) collective-permute-start(bf16[16,80,128]{2,1,0:T(8,128)(2,1)S(1)} %bitcast.247), channel_id=1, source_target_pairs={{0,24},{8,0},{16,8},{24,16},{1,25},{9,1},{17,9},{25,17},{2,26},{10... | collective-permute-start | bytes 983048 | tf_op jit(solution)/shard_map/ppermute | solution.py:245
  159.6 16.9 %collective-permute-start.49 = (bf16[224,448]{1,0:T(8,128)(2,1)S(1)}, bf16[224,448]{1,0:T(8,128)(2,1)S(1)}, u32[]{:S(2)}, u32[]{:S(2)}) collective-permute-start(bf16[224,448]{1,0:T(8,128)(2,1)S(1)} %convolution_convert_fusion.18), channel_id=1, source_target_pairs={{0,24},{8,0},{16,8},{24,16},{1,25},{9,1},{17,9},{25,17},{2,26},{10... | collective-permute-start | bytes 602120 | tf_op jit(solution)/shard_map/ppermute | solution.py:245
  159.8 17.3 %collective-permute-start.48 = (bf16[224,448]{1,0:T(8,128)(2,1)S(1)}, bf16[224,448]{1,0:T(8,128)(2,1)S(1)}, u32[]{:S(2)}, u32[]{:S(2)}) collective-permute-start(bf16[224,448]{1,0:T(8,128)(2,1)S(1)} %convolution_convert_fusion.19), channel_id=1, source_target_pairs={{0,16},{8,24},{16,0},{24,8},{1,17},{9,25},{17,1},{25,9},{2,18},{10... | collective-permute-start | bytes 602120 | tf_op jit(solution)/shard_map/ppermute | solution.py:245
  161.2 16.3 %collective-permute-start.47 = (bf16[224,448]{1,0:T(8,128)(2,1)S(1)}, bf16[224,448]{1,0:T(8,128)(2,1)S(1)}, u32[]{:S(2)}, u32[]{:S(2)}) collective-permute-start(bf16[224,448]{1,0:T(8,128)(2,1)S(1)} %convolution_convert_fusion.20), channel_id=1, source_target_pairs={{0,8},{8,16},{16,24},{24,0},{1,9},{9,17},{17,25},{25,1},{2,10},{10... | collective-permute-start | bytes 602120 | tf_op jit(solution)/shard_map/ppermute | solution.py:245
  162.1 18.5 %collective-permute-start.67 = (bf16[224,448]{1,0:T(8,128)(2,1)S(1)}, bf16[224,448]{1,0:T(8,128)(2,1)S(1)}, u32[]{:S(2)}, u32[]{:S(2)}) collective-permute-start(bf16[224,448]{1,0:T(8,128)(2,1)S(1)} %convolution_convert_fusion.14), channel_id=1, source_target_pairs={{0,6},{2,0},{4,2},{6,4},{1,7},{3,1},{5,3},{7,5},{8,14},{10,8},{12,... | collective-permute-start | bytes 602120 | tf_op jit(solution)/shard_map/ppermute | solution.py:245
  206.0 20.6 %collective-permute-start.28 = (bf16[16,80,128]{2,1,0:T(8,128)(2,1)S(1)}, bf16[16,80,128]{2,1,0:T(8,128)(2,1)S(1)}, u32[]{:S(2)}, u32[]{:S(2)}) collective-permute-start(bf16[16,80,128]{2,1,0:T(8,128)(2,1)S(1)} %bitcast.246), channel_id=1, source_target_pairs={{0,16},{8,24},{16,0},{24,8},{1,17},{9,25},{17,1},{25,9},{2,18},{10... | collective-permute-start | bytes 983048 | tf_op jit(solution)/shard_map/ppermute | solution.py:245
  206.1 23.2 %collective-permute-start.27 = (bf16[16,80,128]{2,1,0:T(8,128)(2,1)S(1)}, bf16[16,80,128]{2,1,0:T(8,128)(2,1)S(1)}, u32[]{:S(2)}, u32[]{:S(2)}) collective-permute-start(bf16[16,80,128]{2,1,0:T(8,128)(2,1)S(1)} %bitcast.245), channel_id=1, source_target_pairs={{0,8},{8,16},{16,24},{24,0},{1,9},{9,17},{17,25},{25,1},{2,10},{10... | collective-permute-start | bytes 983048 | tf_op jit(solution)/shard_map/ppermute | solution.py:245
  206.9 16.0 %collective-permute-start.72 = (bf16[14,448]{1,0:T(8,128)(2,1)S(1)}, bf16[14,448]{1,0:T(8,128)(2,1)S(1)}, u32[]{:S(2)}, u32[]{:S(2)}) collective-permute-start(bf16[14,448]{1,0:T(8,128)(2,1)S(1)} %get-tuple-element.96), channel_id=1, source_target_pairs={{0,16},{8,24},{16,0},{24,8},{1,17},{9,25},{17,1},{25,9},{2,18},{10... | collective-permute-start | bytes 37640 | tf_op jit(solution)/shard_map/ppermute | solution.py:245
  209.7 15.4 %collective-permute-start.71 = (bf16[14,448]{1,0:T(8,128)(2,1)S(1)}, bf16[14,448]{1,0:T(8,128)(2,1)S(1)}, u32[]{:S(2)}, u32[]{:S(2)}) collective-permute-start(bf16[14,448]{1,0:T(8,128)(2,1)S(1)} %get-tuple-element.94), channel_id=1, source_target_pairs={{0,8},{8,16},{16,24},{24,0},{1,9},{9,17},{17,25},{25,1},{2,10},{10... | collective-permute-start | bytes 37640 | tf_op jit(solution)/shard_map/ppermute | solution.py:245
  225.4 17.1 %collective-permute-start.18 = (bf16[16,80,128]{2,1,0:T(8,128)(2,1)S(1)}, bf16[16,80,128]{2,1,0:T(8,128)(2,1)S(1)}, u32[]{:S(2)}, u32[]{:S(2)}) collective-permute-start(bf16[16,80,128]{2,1,0:T(8,128)(2,1)S(1)} %bitcast.242), channel_id=1, source_target_pairs={{0,32},{32,64},{64,96},{96,0},{1,33},{33,65},{65,97},{97,1},{2,34}... | collective-permute-start | bytes 983048 | tf_op jit(solution)/shard_map/ppermute | solution.py:245
  226.5 100.2 %collective-permute-start.76 = (bf16[224,2432]{1,0:T(8,128)(2,1)}, bf16[224,2432]{1,0:T(8,128)(2,1)}, u32[]{:S(2)}, u32[]{:S(2)}) collective-permute-start(bf16[224,2432]{1,0:T(8,128)(2,1)} %convolution_convert_fusion.8), channel_id=1, source_target_pairs={{0,96},{32,0},{64,32},{96,64},{1,97},{33,1},{65,33},{97,65},{2,98}... | collective-permute-start | bytes 3268616 | tf_op jit(solution)/shard_map/ppermute | solution.py:245
  229.5 33.3 %collective-permute-start.32 = (bf16[4,80,128]{2,1,0:T(8,128)(2,1)S(1)}, bf16[4,80,128]{2,1,0:T(8,128)(2,1)S(1)}, u32[]{:S(2)}, u32[]{:S(2)}) collective-permute-start(bf16[4,80,128]{2,1,0:T(8,128)(2,1)S(1)} %get-tuple-element.52), channel_id=1, source_target_pairs={{0,96},{32,0},{64,32},{96,64},{1,97},{33,1},{65,33},{97,65},{2,98}... | collective-permute-start | bytes 245768 | tf_op jit(solution)/shard_map/ppermute | solution.py:245
  237.5 25.8 %collective-permute-start.31 = (bf16[4,80,128]{2,1,0:T(8,128)(2,1)S(1)}, bf16[4,80,128]{2,1,0:T(8,128)(2,1)S(1)}, u32[]{:S(2)}, u32[]{:S(2)}) collective-permute-start(bf16[4,80,128]{2,1,0:T(8,128)(2,1)S(1)} %get-tuple-element.53), channel_id=1, source_target_pairs={{0,64},{32,96},{64,0},{96,32},{1,65},{33,97},{65,1},{97,33},{2,66}... | collective-permute-start | bytes 245768 | tf_op jit(solution)/shard_map/ppermute | solution.py:245
  237.7 25.6 %collective-permute-start.30 = (bf16[4,80,128]{2,1,0:T(8,128)(2,1)S(1)}, bf16[4,80,128]{2,1,0:T(8,128)(2,1)S(1)}, u32[]{:S(2)}, u32[]{:S(2)}) collective-permute-start(bf16[4,80,128]{2,1,0:T(8,128)(2,1)S(1)} %get-tuple-element.54), channel_id=1, source_target_pairs={{0,32},{32,64},{64,96},{96,0},{1,33},{33,65},{65,97},{97,1},{2,34}... | collective-permute-start | bytes 245768 | tf_op jit(solution)/shard_map/ppermute | solution.py:245
  242.7 20.7 %collective-permute-start.23 = (bf16[4,80,128]{2,1,0:T(8,128)(2,1)S(1)}, bf16[4,80,128]{2,1,0:T(8,128)(2,1)S(1)}, u32[]{:S(2)}, u32[]{:S(2)}) collective-permute-start(bf16[4,80,128]{2,1,0:T(8,128)(2,1)S(1)} %get-tuple-element.48), channel_id=1, source_target_pairs={{0,24},{8,0},{16,8},{24,16},{1,25},{9,1},{17,9},{25,17},{2,26},{10... | collective-permute-start | bytes 245768 | tf_op jit(solution)/shard_map/ppermute | solution.py:245
  302.9 28.6 %collective-permute-start.75 = (bf16[224,2432]{1,0:T(8,128)(2,1)}, bf16[224,2432]{1,0:T(8,128)(2,1)S(1)}, u32[]{:S(2)}, u32[]{:S(2)}) collective-permute-start(bf16[224,2432]{1,0:T(8,128)(2,1)} %convolution_convert_fusion.9), channel_id=1, source_target_pairs={{0,64},{32,96},{64,0},{96,32},{1,65},{33,97},{65,1},{97,33},{2,66}... | collective-permute-start | bytes 3268616 | tf_op jit(solution)/shard_map/ppermute | solution.py:245
  318.9 35.2 %collective-permute-start.74 = (bf16[224,2432]{1,0:T(8,128)(2,1)}, bf16[224,2432]{1,0:T(8,128)(2,1)S(1)}, u32[]{:S(2)}, u32[]{:S(2)}) collective-permute-start(bf16[224,2432]{1,0:T(8,128)(2,1)} %convolution_convert_fusion.10), channel_id=1, source_target_pairs={{0,32},{32,64},{64,96},{96,0},{1,33},{33,65},{65,97},{97,1},{2,34}... | collective-permute-start | bytes 3268616 | tf_op jit(solution)/shard_map/ppermute | solution.py:245
  321.7 33.9 %collective-permute-start.85 = (bf16[224,2432]{1,0:T(8,128)(2,1)}, bf16[224,2432]{1,0:T(8,128)(2,1)S(1)}, u32[]{:S(2)}, u32[]{:S(2)}) collective-permute-start(bf16[224,2432]{1,0:T(8,128)(2,1)} %convolution_convert_fusion.4), channel_id=1, source_target_pairs={{0,24},{8,0},{16,8},{24,16},{1,25},{9,1},{17,9},{25,17},{2,26},{10... | collective-permute-start | bytes 3268616 | tf_op jit(solution)/shard_map/ppermute | solution.py:245
  325.0 33.2 %collective-permute-start.84 = (bf16[224,2432]{1,0:T(8,128)(2,1)}, bf16[224,2432]{1,0:T(8,128)(2,1)S(1)}, u32[]{:S(2)}, u32[]{:S(2)}) collective-permute-start(bf16[224,2432]{1,0:T(8,128)(2,1)} %convolution_convert_fusion.5), channel_id=1, source_target_pairs={{0,16},{8,24},{16,0},{24,8},{1,17},{9,25},{17,1},{25,9},{2,18},{10... | collective-permute-start | bytes 3268616 | tf_op jit(solution)/shard_map/ppermute | solution.py:245
  326.7 49.4 %collective-permute-start.83 = (bf16[224,2432]{1,0:T(8,128)(2,1)}, bf16[224,2432]{1,0:T(8,128)(2,1)S(1)}, u32[]{:S(2)}, u32[]{:S(2)}) collective-permute-start(bf16[224,2432]{1,0:T(8,128)(2,1)} %convolution_convert_fusion.6), channel_id=1, source_target_pairs={{0,8},{8,16},{16,24},{24,0},{1,9},{9,17},{17,25},{25,1},{2,10},{10... | collective-permute-start | bytes 3268616 | tf_op jit(solution)/shard_map/ppermute | solution.py:245
  331.6 46.1 %collective-permute-start.94 = (bf16[224,2432]{1,0:T(8,128)(2,1)}, bf16[224,2432]{1,0:T(8,128)(2,1)S(1)}, u32[]{:S(2)}, u32[]{:S(2)}) collective-permute-start(bf16[224,2432]{1,0:T(8,128)(2,1)} %convolution_convert_fusion), channel_id=1, source_target_pairs={{0,6},{2,0},{4,2},{6,4},{1,7},{3,1},{5,3},{7,5},{8,14},{10,8},{12,... | collective-permute-start | bytes 3268616 | tf_op jit(solution)/shard_map/ppermute | solution.py:245
  354.1 28.4 %collective-permute-start.93 = (bf16[224,2432]{1,0:T(8,128)(2,1)S(1)}, bf16[224,2432]{1,0:T(8,128)(2,1)S(1)}, u32[]{:S(2)}, u32[]{:S(2)}) collective-permute-start(bf16[224,2432]{1,0:T(8,128)(2,1)S(1)} %copy-done.21), channel_id=1, source_target_pairs={{0,4},{2,6},{4,0},{6,2},{1,5},{3,7},{5,1},{7,3},{8,12},{10,14},{12... | collective-permute-start | bytes 3268616 | tf_op jit(solution)/shard_map/ppermute | solution.py:245
  355.6 49.3 %collective-permute-start.92 = (bf16[224,2432]{1,0:T(8,128)(2,1)S(1)}, bf16[224,2432]{1,0:T(8,128)(2,1)S(1)}, u32[]{:S(2)}, u32[]{:S(2)}) collective-permute-start(bf16[224,2432]{1,0:T(8,128)(2,1)S(1)} %copy-done.20), channel_id=1, source_target_pairs={{0,2},{2,4},{4,6},{6,0},{1,3},{3,5},{5,7},{7,1},{8,10},{10,12},{12... | collective-permute-start | bytes 3268616 | tf_op jit(solution)/shard_map/ppermute | solution.py:245
  358.2 48.7 %collective-permute-start.79 = (bf16[56,2432]{1,0:T(8,128)(2,1)S(1)}, bf16[56,2432]{1,0:T(8,128)(2,1)S(1)}, u32[]{:S(2)}, u32[]{:S(2)}) collective-permute-start(bf16[56,2432]{1,0:T(8,128)(2,1)S(1)} %get-tuple-element.41), channel_id=1, source_target_pairs={{0,24},{8,0},{16,8},{24,16},{1,25},{9,1},{17,9},{25,17},{2,26},{10... | collective-permute-start | bytes 817160 | tf_op jit(solution)/shard_map/ppermute | solution.py:245
  376.1 30.9 %collective-permute-start.78 = (bf16[56,2432]{1,0:T(8,128)(2,1)S(1)}, bf16[56,2432]{1,0:T(8,128)(2,1)S(1)}, u32[]{:S(2)}, u32[]{:S(2)}) collective-permute-start(bf16[56,2432]{1,0:T(8,128)(2,1)S(1)} %get-tuple-element.42), channel_id=1, source_target_pairs={{0,16},{8,24},{16,0},{24,8},{1,17},{9,25},{17,1},{25,9},{2,18},{10... | collective-permute-start | bytes 817160 | tf_op jit(solution)/shard_map/ppermute | solution.py:245
  377.7 29.7 %collective-permute-start.77 = (bf16[56,2432]{1,0:T(8,128)(2,1)S(1)}, bf16[56,2432]{1,0:T(8,128)(2,1)S(1)}, u32[]{:S(2)}, u32[]{:S(2)}) collective-permute-start(bf16[56,2432]{1,0:T(8,128)(2,1)S(1)} %get-tuple-element.43), channel_id=1, source_target_pairs={{0,8},{8,16},{16,24},{24,0},{1,9},{9,17},{17,25},{25,1},{2,10},{10... | collective-permute-start | bytes 817160 | tf_op jit(solution)/shard_map/ppermute | solution.py:245
  382.5 28.3 %collective-permute-start.88 = (bf16[56,2432]{1,0:T(8,128)(2,1)S(1)}, bf16[56,2432]{1,0:T(8,128)(2,1)S(1)}, u32[]{:S(2)}, u32[]{:S(2)}) collective-permute-start(bf16[56,2432]{1,0:T(8,128)(2,1)S(1)} %get-tuple-element.37), channel_id=1, source_target_pairs={{0,6},{2,0},{4,2},{6,4},{1,7},{3,1},{5,3},{7,5},{8,14},{10,8},{12,... | collective-permute-start | bytes 817160 | tf_op jit(solution)/shard_map/ppermute | solution.py:245
  407.1 15.4 %collective-permute-start.97 = (bf16[56,2432]{1,0:T(8,128)(2,1)S(1)}, bf16[56,2432]{1,0:T(8,128)(2,1)S(1)}, u32[]{:S(2)}, u32[]{:S(2)}) collective-permute-start(bf16[56,2432]{1,0:T(8,128)(2,1)S(1)} %get-tuple-element.33), channel_id=1, source_target_pairs={{0,96},{32,0},{64,32},{96,64},{1,97},{33,1},{65,33},{97,65},{2,98}... | collective-permute-start | bytes 817160 | tf_op jit(solution)/shard_map/ppermute | solution.py:245
  407.4 15.2 %collective-permute-start.96 = (bf16[56,2432]{1,0:T(8,128)(2,1)S(1)}, bf16[56,2432]{1,0:T(8,128)(2,1)S(1)}, u32[]{:S(2)}, u32[]{:S(2)}) collective-permute-start(bf16[56,2432]{1,0:T(8,128)(2,1)S(1)} %get-tuple-element.34), channel_id=1, source_target_pairs={{0,64},{32,96},{64,0},{96,32},{1,65},{33,97},{65,1},{97,33},{2,66}... | collective-permute-start | bytes 817160 | tf_op jit(solution)/shard_map/ppermute | solution.py:245
  (113 other events, 1239.5 us)
